TPU v7x, 32 devices: a whole 2x2x4 slice. The times are simulated.
32 devices in a mesh: acq: 4 (over y, core), tile: 8 (over z, x).
Axes of the slice: x: 2, y: 2, z: 4, core: 2. Of those that a mesh axis runs over, the one named last changes fastest.
Arguments:
- slc: bfloat16 [32, 2, 64, 8192], P(('acq', 'tile'))
- offsets: int32 [32, 64], replicated, may hold values from -256 to 255
- partners: int32 [32, 4], replicated, may hold values from 0 to 31, as said below
Outputs:
- interferogram: float32 [2, 32, 4, 16, 512], P(None, 'acq', None, None, 'tile')
- coherence: float32 [32, 4, 16, 512], P('acq', None, None, 'tile')
Inputs may be any that keep to these rules, and one draw needn't show every extreme that they name: partners[i, k] differs from i by 1 to 6; some pair of every draw lies exactly 6 acquisitions forward and some exactly 6 backward.
All inputs are finite; a program needn't handle non-finite values.
Results may differ from a plain program's by a relative error of at most 0.003.
Values may be sent and summed in bfloat16 or wider, within the bound.
A program may use at most 128 MiB of HBM per device.

v0:
```python
import functools

import jax
import jax.numpy as jnp
import numpy as np
from jax import lax
from jax.experimental import pallas as pl
from jax.experimental.pallas import tpu as pltpu
from jax.sharding import PartitionSpec as P

MAXGAP = 6
TAPS = 8
PHASES = 64
LA = 4
LR = 16
LANES = 128
CHUNKS = 4
STRIP = 512
DEVICE = pl.DeviceIdType.MESH


def offset_table():
    spot = np.arange(TAPS)[None, :] - (TAPS // 2 - 1) - np.arange(PHASES)[:, None] / PHASES
    raw = np.sinc(spot) * 0.5 * (1.0 + np.cos(np.pi * spot / (TAPS // 2)))
    kernel = raw / raw.sum(axis=1, keepdims=True)
    table = np.zeros((TAPS * PHASES, LANES), np.float32)
    for row in range(TAPS * PHASES):
        whole = row // PHASES - TAPS // 2
        first = whole + TAPS // 2
        table[row, first : first + TAPS] = kernel[row % PHASES]
    return table


def flipped(index, mask, size):
    out = 0
    bit = 1
    while bit < size:
        out = out + ((index // bit + mask // bit) % 2) * bit
        bit *= 2
    return out


def weighted_shifts(window, weights):
    width = window.shape[1]

    def ahead(value, count):
        return value if count == 0 else pltpu.roll(value, (-count) % width, 1)

    near = [ahead(window, s) for s in (-1, 0, 1)]
    total = None
    for q in (-2, -1, 0, 1, 2):
        part = None
        for s in (-1, 0, 1):
            weight = weights(3 * q + s + TAPS - 1)
            term = near[s + 1] * weight
            part = term if part is None else part + term
        part = ahead(part, 3 * q)
        total = part if total is None else total + part
    return total


def kernel(
    offsets_ref, table_ref, partners_ref, slc_ref, looked_ref, coherent_ref,
    padded, weights, outgoing, pool, pool_power, cross_sum, power_sum, *rest,
):
    extended = rest[:CHUNKS]
    in_sem, own_sem, send_sem, recv_sem, up_send, up_recv, down_send, down_recv = rest[CHUNKS:]
    group = lax.axis_size("tile")
    groups = lax.axis_size("acq")
    tile = lax.axis_index("tile")
    acq = lax.axis_index("acq")
    parts, az_rows, rg_cols = slc_ref.shape[1:]
    cols = rg_cols // group
    width = cols // CHUNKS
    looks = cols // LR
    slots = group + 2 * MAXGAP
    has_down, has_up = acq > 0, acq < groups - 1

    load = pltpu.make_async_copy(slc_ref.at[0], padded.at[:, :, pl.ds(LANES, rg_cols)], in_sem)
    load.start()

    barrier = pltpu.get_barrier_semaphore()

    def greet(step, carry):
        other = flipped(tile, group - 1 - step, group)
        pl.semaphore_signal(barrier, inc=1, device_id=(acq, other), device_id_type=DEVICE)
        return carry

    lax.fori_loop(0, group - 1, greet, 0)

    @pl.when(has_down)
    def _():
        pl.semaphore_signal(barrier, inc=1, device_id=(acq - 1, tile), device_id_type=DEVICE)

    @pl.when(has_up)
    def _():
        pl.semaphore_signal(barrier, inc=1, device_id=(acq + 1, tile), device_id_type=DEVICE)

    own = offsets_ref[pl.ds(acq * group + tile, 1), :]
    rows = lax.broadcasted_iota(jnp.int32, (TAPS * PHASES, az_rows), 0)
    onehot = jnp.where(rows == own + TAPS // 2 * PHASES, 1.0, 0.0).astype(jnp.float32)
    found = lax.dot_general(
        onehot, table_ref[...], (((0,), (0,)), ((), ())),
        precision=lax.Precision.HIGHEST, preferred_element_type=jnp.float32,
    )
    for d in range(2 * TAPS - 1):
        weights[d] = jnp.broadcast_to(found[:, d : d + 1], (az_rows, LANES))
    edge = jnp.zeros((parts, az_rows, LANES), padded.dtype)
    padded[:, :, pl.ds(0, LANES)] = edge
    padded[:, :, pl.ds(LANES + rg_cols, LANES)] = edge

    load.wait()

    greeted = jnp.where(has_down, 1, 0) + jnp.where(has_up, 1, 0)
    pl.semaphore_wait(barrier, group - 1 + greeted)

    def to_tile(step, chunk, other):
        return pltpu.make_async_remote_copy(
            src_ref=outgoing.at[step, chunk],
            dst_ref=extended[chunk].at[MAXGAP + tile],
            send_sem=send_sem.at[chunk, step],
            recv_sem=recv_sem.at[chunk, tile],
            device_id=(acq, other),
            device_id_type=DEVICE,
        )

    def from_tile(step, chunk, other):
        return pltpu.make_async_remote_copy(
            src_ref=outgoing.at[step, chunk],
            dst_ref=extended[chunk].at[MAXGAP + other],
            send_sem=send_sem.at[chunk, step],
            recv_sem=recv_sem.at[chunk, other],
            device_id=(acq, other),
            device_id_type=DEVICE,
        )

    def keep(chunk):
        return pltpu.make_async_copy(
            outgoing.at[group - 1, chunk], extended[chunk].at[MAXGAP + tile], own_sem.at[chunk]
        )

    def resample(step, carry):
        other = flipped(tile, group - 1 - step, group)
        begin = pl.multiple_of(other * cols, LANES)

        def row_block(index, inner):
            part = index // (az_rows // 16)
            row = pl.multiple_of(index % (az_rows // 16) * 16, 16)
            for strip in range(cols // STRIP):
                start = pl.multiple_of(begin + strip * STRIP, LANES)
                span = STRIP + 2 * LANES
                window = padded[part, pl.ds(row, 16), pl.ds(start, span)].astype(jnp.float32)

                def weight(d):
                    return jnp.concatenate([weights[d, pl.ds(row, 16), :]] * (span // LANES), axis=1)

                total = weighted_shifts(window, weight)[:, LANES : LANES + STRIP].astype(jnp.bfloat16)
                for piece in range(STRIP // width):
                    outgoing[step, strip * (STRIP // width) + piece, part, pl.ds(row, 16), :] = total[
                        :, piece * width : (piece + 1) * width
                    ]
            return inner

        lax.fori_loop(0, parts * (az_rows // 16), row_block, 0)

        @pl.when(step < group - 1)
        def _():
            to_tile(step, 0, other).start()

        return carry

    lax.fori_loop(0, group, resample, 0)
    for chunk in range(CHUNKS):
        keep(chunk).start()
        if chunk:

            def send(step, carry, chunk=chunk):
                to_tile(step, chunk, flipped(tile, group - 1 - step, group)).start()
                return carry

            lax.fori_loop(0, group - 1, send, 0)

    for chunk in range(CHUNKS):
        for quarter in range(4):
            spot = (lax.broadcasted_iota(jnp.int32, (width, 2 * looks), 0) + chunk * width) // LR
            lane = lax.broadcasted_iota(jnp.int32, (width, 2 * looks), 1)
            hit = jnp.where(lane == spot + (looks if quarter >= 2 else 0), 1.0, 0.0)
            pool[chunk, quarter * width : (quarter + 1) * width] = (
                -hit if quarter == 3 else hit
            ).astype(jnp.bfloat16)
            if quarter < 2:
                both = jnp.where((lane == spot) | (lane == spot + looks), 1.0, 0.0)
                pool_power[chunk, quarter * width : (quarter + 1) * width] = both.astype(jnp.bfloat16)

    def up(chunk, source):
        return pltpu.make_async_remote_copy(
            src_ref=extended[chunk].at[MAXGAP + source],
            dst_ref=extended[chunk].at[source - (group - MAXGAP)],
            send_sem=up_send.at[chunk, source - (group - MAXGAP)],
            recv_sem=up_recv.at[chunk, source - (group - MAXGAP)],
            device_id=(acq + 1, tile),
            device_id_type=DEVICE,
        )

    def down(chunk, source):
        return pltpu.make_async_remote_copy(
            src_ref=extended[chunk].at[MAXGAP + source],
            dst_ref=extended[chunk].at[MAXGAP + group + source],
            send_sem=down_send.at[chunk, source],
            recv_sem=down_recv.at[chunk, source],
            device_id=(acq - 1, tile),
            device_id_type=DEVICE,
        )

    def hand_on(chunk, source):
        @pl.when(has_up & (source >= group - MAXGAP))
        def _():
            up(chunk, source).start()

        @pl.when(has_down & (source < MAXGAP))
        def _():
            down(chunk, source).start()

    def relay(chunk):
        keep(chunk).wait()
        hand_on(chunk, tile)

        def one(index, carry):
            step = group - 2 - index
            source = flipped(tile, group - 1 - step, group)
            from_tile(step, chunk, source).wait_recv()
            hand_on(chunk, source)
            return carry

        lax.fori_loop(0, group - 1, one, 0)

    def gathered(chunk):
        @pl.when(has_down)
        def _():
            def one(index, carry):
                up(chunk, index + group - MAXGAP).wait_recv()
                return carry

            lax.fori_loop(0, MAXGAP, one, 0)

        @pl.when(has_up)
        def _():
            def one(index, carry):
                down(chunk, index).wait_recv()
                return carry

            lax.fori_loop(0, MAXGAP, one, 0)

    def slot_of(owner, k):
        return jnp.clip(partners_ref[acq * group + owner, k] - acq * group + MAXGAP, 0, slots - 1)

    def pairs(chunk):
        images = extended[chunk]

        def powers(index, carry):
            squares = []
            for k in range(4):
                image = images[index * 4 + k]
                squares.append(jnp.concatenate([image[0] * image[0], image[1] * image[1]], axis=1))
            pooled = jnp.dot(
                jnp.concatenate(squares, axis=0), pool_power[chunk], preferred_element_type=jnp.float32
            ).reshape(4, az_rows, 2 * looks)
            span = pl.ds(index * 4, 4)
            power_sum[span] = pooled if chunk == 0 else power_sum[span] + pooled
            return carry

        lax.fori_loop(0, slots // 4, powers, 0)

        def crosses(owner, carry):
            first = images[MAXGAP + owner]
            blocks = []
            for k in range(partners_ref.shape[1]):
                second = images[slot_of(owner, k)]
                blocks.append(
                    jnp.concatenate(
                        [first[0] * second[0], first[1] * second[1], first[1] * second[0], first[0] * second[1]],
                        axis=1,
                    )
                )
            pooled = jnp.dot(
                jnp.concatenate(blocks, axis=0), pool[chunk], preferred_element_type=jnp.float32
            ).reshape(len(blocks), az_rows, 2 * looks)
            cross_sum[owner] = pooled if chunk == 0 else cross_sum[owner] + pooled
            return carry

        lax.fori_loop(0, group, crosses, 0)

    relay(0)
    for chunk in range(CHUNKS):
        gathered(chunk)
        pairs(chunk)
        if chunk + 1 < CHUNKS:
            relay(chunk + 1)

    windows = az_rows // LA

    def mean(view, *lead):
        total = None
        for line in range(LA):
            value = view[(*lead, pl.ds(line, windows, stride=LA), slice(None))]
            total = value if total is None else total + value
        return total * (1.0 / (LA * LR))

    def finish(owner, carry):
        mean_a = mean(power_sum, MAXGAP + owner)
        for k in range(partners_ref.shape[1]):
            mean_b = mean(power_sum, slot_of(owner, k))
            cross = mean(cross_sum, owner, k)
            square = cross * cross
            magnitude = jnp.sqrt(square + pltpu.roll(square, looks, 1))
            coherent = magnitude / jnp.sqrt((mean_a + 1e-06) * (mean_b + 1e-06))
            looked_ref[0, owner, k] = cross[:, :looks]
            looked_ref[1, owner, k] = pltpu.roll(cross, looks, 1)[:, :looks]
            coherent_ref[owner, k] = coherent[:, :looks]
        return carry

    lax.fori_loop(0, group, finish, 0)

    for chunk in range(CHUNKS):

        def sent(step, carry, chunk=chunk):
            to_tile(step, chunk, flipped(tile, group - 1 - step, group)).wait_send()
            return carry

        lax.fori_loop(0, group - 1, sent, 0)

        @pl.when(has_up)
        def _(chunk=chunk):
            def one(index, carry):
                up(chunk, index + group - MAXGAP).wait_send()
                return carry

            lax.fori_loop(0, MAXGAP, one, 0)

        @pl.when(has_down)
        def _(chunk=chunk):
            def one(index, carry):
                down(chunk, index).wait_send()
                return carry

            lax.fori_loop(0, MAXGAP, one, 0)


def body(group, slc, offsets, partners):
    _, parts, az_rows, rg_cols = slc.shape
    pair_count = partners.shape[1]
    cols = rg_cols // group
    width, looks = cols // CHUNKS, cols // LR
    slots = group + 2 * MAXGAP
    vmem = pl.BlockSpec(memory_space=pltpu.VMEM)
    dma = pltpu.SemaphoreType.DMA
    return pl.pallas_call(
        kernel,
        out_shape=(
            jax.ShapeDtypeStruct((2, group, pair_count, az_rows // LA, looks), jnp.float32),
            jax.ShapeDtypeStruct((group, pair_count, az_rows // LA, looks), jnp.float32),
        ),
        in_specs=[vmem, vmem, pl.BlockSpec(memory_space=pltpu.SMEM), pl.BlockSpec(memory_space=pl.ANY)],
        out_specs=(vmem, vmem),
        scratch_shapes=[
            pltpu.VMEM((parts, az_rows, rg_cols + 2 * LANES), jnp.bfloat16),
            pltpu.VMEM((2 * TAPS - 1, az_rows, LANES), jnp.float32),
            pltpu.VMEM((group, CHUNKS, parts, az_rows, width), jnp.bfloat16),
            pltpu.VMEM((CHUNKS, 4 * width, 2 * looks), jnp.bfloat16),
            pltpu.VMEM((CHUNKS, 2 * width, 2 * looks), jnp.bfloat16),
            pltpu.VMEM((group, pair_count, az_rows, 2 * looks), jnp.float32),
            pltpu.VMEM((slots, az_rows, 2 * looks), jnp.float32),
        ]
        + [pltpu.VMEM((slots, parts, az_rows, width), jnp.bfloat16)] * CHUNKS
        + [
            dma(()),
            dma((CHUNKS,)),
            dma((CHUNKS, group)),
            dma((CHUNKS, group)),
            dma((CHUNKS, MAXGAP)),
            dma((CHUNKS, MAXGAP)),
            dma((CHUNKS, MAXGAP)),
            dma((CHUNKS, MAXGAP)),
        ],
        compiler_params=pltpu.CompilerParams(
            collective_id=0, has_side_effects=True, vmem_limit_bytes=48 * 1024 * 1024
        ),
    )(offsets, jnp.asarray(offset_table()), partners, slc)


def solution(mesh):
    return jax.shard_map(
        functools.partial(body, mesh.shape["tile"]),
        mesh=mesh,
        in_specs=(P(("acq", "tile"), None, None, None), P(), P()),
        out_specs=(P(None, "acq", None, None, "tile"), P("acq", None, None, "tile")),
        check_vma=False,
    )
```

profile of v0, /device:TPU:1, one launch (start us, length us, event | category | flops | bytes accessed | tf_op | source)
XLA Modules:
  0.0 81.1 jit_solution(2841104577613240973)
XLA Ops:
  0.6 0.8 copy.6.partners_ref
  1.4 0.0 copy-start
  1.4 1.6 %copy-done = bf16[1,2,64,8192]{3,2,1,0:T(8,128)(2,1)S(1)} copy-done((bf16[1,2,64,8192]{3,2,1,0:T(8,128)(2,1)S(1)}, bf16[1,2,64,8192]{3,2,1,0:T(8,128)(2,1)}, u32[]{:S(2)}) %copy-start) | copy-done | bytes 2097176
  3.0 0.0 copy-start.1
  3.0 0.9 %copy-done.1 = f32[512,128]{1,0:T(8,128)S(1)} copy-done((f32[512,128]{1,0:T(8,128)S(1)}, f32[512,128]{1,0:T(8,128)}, u32[]{:S(2)}) %copy-start.1) | copy-done | bytes 262168
  3.9 0.0 copy-start.2
  3.9 0.7 copy-done.2
  4.7 74.9 %shard_map.59 = (f32[2,8,4,16,64]{4,3,2,1,0:T(8,128)S(1)}, f32[8,4,16,64]{3,2,1,0:T(8,128)S(1)}) custom-call(s32[32,64]{1,0:T(8,128)S(1)} %copy-done.2, f32[512,128]{1,0:T(8,128)S(1)} %copy-done.1, s32[32,4]{1,0:T(8,128)S(1)} %copy.6.partners_ref, bf16[1,2,64,8192]{3,2,1,0:T(8,128)(2,1)S(1)} %copy-done), custom_call_target="tpu_custom_call" | custom-call | tf_op jit(solution)/shard_map/pallas_call | solution.py:357
  79.6 0.8 copy.9
  80.4 0.7 copy.10
Async XLA Ops:
  1.4 1.6 %copy-start = (bf16[1,2,64,8192]{3,2,1,0:T(8,128)(2,1)S(1)}, bf16[1,2,64,8192]{3,2,1,0:T(8,128)(2,1)}, u32[]{:S(2)}) copy-start(bf16[1,2,64,8192]{3,2,1,0:T(8,128)(2,1)} %slc_ref.1) | copy-start | bytes 6291460
  3.0 0.9 %copy-start.1 = (f32[512,128]{1,0:T(8,128)S(1)}, f32[512,128]{1,0:T(8,128)}, u32[]{:S(2)}) copy-start(f32[512,128]{1,0:T(8,128)} %constant.2.clone.table_ref) | copy-start | bytes 786436
  3.9 0.7 copy-start.2
where the time goes:
time: 81.3 us; the launch traced here: 81.1 us
  Pallas kernels  74.9 us (92%)
  local copies, waits for them, and re-layouts  5.52 us (7%)
    pallas_call x1, Pallas kernels, body(): pl.pallas_call(kernel, out_shape=(jax.ShapeDtypeStruct((2, group, pair_co...  74.9 us
    unnamed x9, local copies, waits for them, and re-layouts  5.52 us

commit v1 on v0

v1 whole, which is shorter than its diff:
```python
import functools

import jax
import jax.numpy as jnp
from jax import lax
from jax.experimental import pallas as pl
from jax.experimental.pallas import tpu as pltpu
from jax.sharding import PartitionSpec as P

MAXGAP = 6
TAPS = 8
PHASES = 64
LA = 4
LR = 16
LANES = 128
SHARES = (1, 1, 1, 1)
CHUNKS = len(SHARES)
EARLY = 1
OWNERS = 4
DEVICE = pl.DeviceIdType.MESH


def chunk_spans(cols):
    unit = cols // sum(SHARES)
    return [(sum(SHARES[:c]) * unit, SHARES[c] * unit) for c in range(CHUNKS)]


def flipped(index, mask, size):
    out = 0
    bit = 1
    while bit < size:
        out = out + ((index // bit + mask // bit) % 2) * bit
        bit *= 2
    return out


def weighted_shifts(window, weights):
    width = window.shape[1]

    def ahead(value, count):
        return value if count == 0 else pltpu.roll(value, (-count) % width, 1)

    near = [ahead(window, s) for s in (-1, 0, 1)]
    total = None
    for q in (-2, -1, 0, 1, 2):
        part = None
        for s in (-1, 0, 1):
            weight = weights(3 * q + s + TAPS - 1)
            term = near[s + 1] * weight
            part = term if part is None else part + term
        part = ahead(part, 3 * q)
        total = part if total is None else total + part
    return total


def kernel(
    offsets_ref, partners_ref, slc_ref, looked_ref, coherent_ref,
    offsets, padded, weights, cross_sum, power_sum, *rest,
):
    extended, outgoing, pool, pool_power = (rest[i * CHUNKS : (i + 1) * CHUNKS] for i in range(4))
    fetch_sem, in_sem, own_sem, send_sem, recv_sem, up_send, up_recv, down_send, down_recv = rest[4 * CHUNKS :]
    group = lax.axis_size("tile")
    groups = lax.axis_size("acq")
    tile = lax.axis_index("tile")
    acq = lax.axis_index("acq")
    parts, az_rows, rg_cols = slc_ref.shape[1:]
    cols = rg_cols // group
    spans = chunk_spans(cols)
    looks = cols // LR
    slots = group + 2 * MAXGAP
    pair_count = partners_ref.shape[0]
    has_down, has_up = acq > 0, acq < groups - 1

    fetch = pltpu.make_async_copy(offsets_ref, offsets, fetch_sem)
    fetch.start()
    load = pltpu.make_async_copy(slc_ref.at[0], padded.at[:, :, pl.ds(LANES, rg_cols)], in_sem)
    load.start()

    barrier = pltpu.get_barrier_semaphore()

    def greet(step, carry):
        other = flipped(tile, group - 1 - step, group)
        pl.semaphore_signal(barrier, inc=1, device_id=(acq, other), device_id_type=DEVICE)
        return carry

    lax.fori_loop(0, group - 1, greet, 0)

    @pl.when(has_down)
    def _():
        pl.semaphore_signal(barrier, inc=1, device_id=(acq - 1, tile), device_id_type=DEVICE)

    @pl.when(has_up)
    def _():
        pl.semaphore_signal(barrier, inc=1, device_id=(acq + 1, tile), device_id_type=DEVICE)

    fetch.wait()
    own = jnp.broadcast_to(
        offsets[pl.ds(acq * group + tile, 1), :].astype(jnp.float32), (az_rows, az_rows)
    )
    diagonal = lax.broadcasted_iota(jnp.int32, (az_rows, az_rows), 0) == lax.broadcasted_iota(
        jnp.int32, (az_rows, az_rows), 1
    )
    own = jnp.sum(jnp.where(diagonal, own, 0.0), axis=1, keepdims=True)
    shift = lax.broadcasted_iota(jnp.int32, (az_rows, LANES), 1) - (TAPS - 1)
    spot = shift.astype(jnp.float32) - own * (1.0 / PHASES)
    angle = jnp.pi * spot
    sinc = jnp.where(spot == 0.0, 1.0, jnp.sin(angle) / jnp.where(spot == 0.0, 1.0, angle))
    raw = sinc * (0.5 * (1.0 + jnp.cos(angle * (2.0 / TAPS))))
    raw = jnp.where(jnp.abs(spot) < TAPS // 2, raw, 0.0)
    found = raw / jnp.sum(raw, axis=1, keepdims=True)
    for d in range(2 * TAPS - 1):
        weights[d] = jnp.broadcast_to(found[:, d : d + 1], (az_rows, LANES))
    edge = jnp.zeros((parts, az_rows, LANES), padded.dtype)
    padded[:, :, pl.ds(0, LANES)] = edge
    padded[:, :, pl.ds(LANES + rg_cols, LANES)] = edge

    load.wait()

    greeted = jnp.where(has_down, 1, 0) + jnp.where(has_up, 1, 0)
    pl.semaphore_wait(barrier, group - 1 + greeted)

    def to_tile(step, chunk, other):
        return pltpu.make_async_remote_copy(
            src_ref=outgoing[chunk].at[step],
            dst_ref=extended[chunk].at[MAXGAP + tile],
            send_sem=send_sem.at[chunk, step],
            recv_sem=recv_sem.at[chunk, tile],
            device_id=(acq, other),
            device_id_type=DEVICE,
        )

    def from_tile(step, chunk, other):
        return pltpu.make_async_remote_copy(
            src_ref=outgoing[chunk].at[step],
            dst_ref=extended[chunk].at[MAXGAP + other],
            send_sem=send_sem.at[chunk, step],
            recv_sem=recv_sem.at[chunk, other],
            device_id=(acq, other),
            device_id_type=DEVICE,
        )

    def keep(chunk):
        return pltpu.make_async_copy(
            outgoing[chunk].at[group - 1], extended[chunk].at[MAXGAP + tile], own_sem.at[chunk]
        )

    def resample(step, carry):
        other = flipped(tile, group - 1 - step, group)
        begin = pl.multiple_of(other * cols, LANES)

        def row_block(index, inner):
            part = index // (az_rows // 16)
            row = pl.multiple_of(index % (az_rows // 16) * 16, 16)
            span = cols + 2 * LANES
            window = padded[part, pl.ds(row, 16), pl.ds(begin, span)].astype(jnp.float32)

            def weight(half, d):
                return jnp.concatenate([weights[d, pl.ds(row + half, 8), :]] * (span // LANES), axis=1)

            total = jnp.concatenate(
                [
                    weighted_shifts(window[:8], functools.partial(weight, 0)),
                    weighted_shifts(window[8:], functools.partial(weight, 8)),
                ],
                axis=0,
            )[:, LANES : LANES + cols].astype(jnp.bfloat16)
            for chunk, (first, width) in enumerate(spans):
                outgoing[chunk][step, part, pl.ds(row, 16), :] = total[:, first : first + width]
            return inner

        lax.fori_loop(0, parts * (az_rows // 16), row_block, 0)

        @pl.when(step < group - 1)
        def _():
            to_tile(step, 0, other).start()

        return carry

    def send(chunk, begin, end):
        def one(step, carry):
            to_tile(group - 2 - step, chunk, flipped(tile, 1 + step, group)).start()
            return carry

        lax.fori_loop(begin, end, one, 0)

    lax.fori_loop(0, group // 2, resample, 0)
    for chunk in range(1, EARLY):
        send(chunk, 0, group // 2)
    lax.fori_loop(group // 2, group, resample, 0)
    for chunk in range(1, CHUNKS):
        send(chunk, group // 2 if chunk < EARLY else 0, group - 1)
    for chunk in range(CHUNKS):
        keep(chunk).start()

    for chunk, (first, width) in enumerate(spans):
        spot = (lax.broadcasted_iota(jnp.int32, (width, 2 * looks), 0) + first) // LR
        lane = lax.broadcasted_iota(jnp.int32, (width, 2 * looks), 1)
        left = jnp.where(lane == spot, 1.0, 0.0)
        right = jnp.where(lane == spot + looks, 1.0, 0.0)
        for quarter, block in enumerate((left, left, right, -right)):
            pool[chunk][quarter * width : (quarter + 1) * width] = block.astype(jnp.bfloat16)
        for half in range(2):
            pool_power[chunk][half * width : (half + 1) * width] = (left + right).astype(jnp.bfloat16)

    def up(chunk, source):
        return pltpu.make_async_remote_copy(
            src_ref=extended[chunk].at[MAXGAP + source],
            dst_ref=extended[chunk].at[source - (group - MAXGAP)],
            send_sem=up_send.at[chunk, source - (group - MAXGAP)],
            recv_sem=up_recv.at[chunk, source - (group - MAXGAP)],
            device_id=(acq + 1, tile),
            device_id_type=DEVICE,
        )

    def down(chunk, source):
        return pltpu.make_async_remote_copy(
            src_ref=extended[chunk].at[MAXGAP + source],
            dst_ref=extended[chunk].at[MAXGAP + group + source],
            send_sem=down_send.at[chunk, source],
            recv_sem=down_recv.at[chunk, source],
            device_id=(acq - 1, tile),
            device_id_type=DEVICE,
        )

    def hand_on(chunk, source):
        @pl.when(has_up & (source >= group - MAXGAP))
        def _():
            up(chunk, source).start()

        @pl.when(has_down & (source < MAXGAP))
        def _():
            down(chunk, source).start()

    def relay(chunk):
        keep(chunk).wait()
        hand_on(chunk, tile)

        def one(index, carry):
            step = group - 2 - index
            source = flipped(tile, group - 1 - step, group)
            from_tile(step, chunk, source).wait_recv()
            hand_on(chunk, source)
            return carry

        lax.fori_loop(0, group - 1, one, 0)

    def gathered(chunk):
        @pl.when(has_down)
        def _():
            def one(index, carry):
                up(chunk, index + group - MAXGAP).wait_recv()
                return carry

            lax.fori_loop(0, MAXGAP, one, 0)

        @pl.when(has_up)
        def _():
            def one(index, carry):
                down(chunk, index).wait_recv()
                return carry

            lax.fori_loop(0, MAXGAP, one, 0)

    def slot_of(owner, k):
        return jnp.clip(partners_ref[k, acq * group + owner] - acq * group + MAXGAP, 0, slots - 1)

    def pairs(chunk):
        images = extended[chunk]

        def powers(index, carry):
            squares = []
            for k in range(4):
                image = images[index * 4 + k]
                squares.append(jnp.concatenate([image[0] * image[0], image[1] * image[1]], axis=1))
            pooled = jnp.dot(
                jnp.concatenate(squares, axis=0), pool_power[chunk][...], preferred_element_type=jnp.float32
            ).reshape(4, az_rows, 2 * looks)
            span = pl.ds(index * 4, 4)
            power_sum[span] = pooled if chunk == 0 else power_sum[span] + pooled
            return carry

        lax.fori_loop(0, slots // 4, powers, 0)

        def crosses(index, carry):
            blocks = []
            for owner in (index * OWNERS + j for j in range(OWNERS)):
                first = images[MAXGAP + owner]
                for k in range(pair_count):
                    second = images[slot_of(owner, k)]
                    blocks.append(
                        jnp.concatenate(
                            [first[0] * second[0], first[1] * second[1], first[1] * second[0], first[0] * second[1]],
                            axis=1,
                        )
                    )
            pooled = jnp.dot(
                jnp.concatenate(blocks, axis=0), pool[chunk][...], preferred_element_type=jnp.float32
            ).reshape(OWNERS, pair_count, az_rows, 2 * looks)
            span = pl.ds(index * OWNERS, OWNERS)
            cross_sum[span] = pooled if chunk == 0 else cross_sum[span] + pooled
            return carry

        lax.fori_loop(0, group // OWNERS, crosses, 0)

    relay(0)
    for chunk in range(CHUNKS):
        if chunk + 1 < CHUNKS:
            relay(chunk + 1)
        gathered(chunk)
        pairs(chunk)

    windows = az_rows // LA

    def mean(view, *lead):
        total = None
        for line in range(LA):
            value = view[(*lead, pl.ds(line, windows, stride=LA), slice(None))]
            total = value if total is None else total + value
        return total * (1.0 / (LA * LR))

    def finish(owner):
        mean_a = mean(power_sum, MAXGAP + owner)
        for k in range(partners_ref.shape[0]):
            mean_b = mean(power_sum, slot_of(owner, k))
            cross = mean(cross_sum, owner, k)
            square = cross * cross
            magnitude = jnp.sqrt(square + pltpu.roll(square, looks, 1))
            coherent = magnitude / jnp.sqrt((mean_a + 1e-06) * (mean_b + 1e-06))
            looked_ref[0, owner, k] = cross[:, :looks]
            looked_ref[1, owner, k] = pltpu.roll(cross, looks, 1)[:, :looks]
            coherent_ref[owner, k] = coherent[:, :looks]

    @pl.loop(0, group // 2)
    def _(index):
        finish(index * 2)
        finish(index * 2 + 1)

    for chunk in range(CHUNKS):

        def sent(step, carry, chunk=chunk):
            to_tile(step, chunk, flipped(tile, group - 1 - step, group)).wait_send()
            return carry

        lax.fori_loop(0, group - 1, sent, 0)

        @pl.when(has_up)
        def _(chunk=chunk):
            def one(index, carry):
                up(chunk, index + group - MAXGAP).wait_send()
                return carry

            lax.fori_loop(0, MAXGAP, one, 0)

        @pl.when(has_down)
        def _(chunk=chunk):
            def one(index, carry):
                down(chunk, index).wait_send()
                return carry

            lax.fori_loop(0, MAXGAP, one, 0)


def body(group, slc, offsets, partners):
    _, parts, az_rows, rg_cols = slc.shape
    pair_count = partners.shape[1]
    cols = rg_cols // group
    looks = cols // LR
    widths = [width for _, width in chunk_spans(cols)]
    slots = group + 2 * MAXGAP
    vmem = pl.BlockSpec(memory_space=pltpu.VMEM)
    hbm = pl.BlockSpec(memory_space=pltpu.HBM)
    dma = pltpu.SemaphoreType.DMA
    return pl.pallas_call(
        kernel,
        out_shape=(
            jax.ShapeDtypeStruct((2, group, pair_count, az_rows // LA, looks), jnp.float32),
            jax.ShapeDtypeStruct((group, pair_count, az_rows // LA, looks), jnp.float32),
        ),
        in_specs=[hbm, pl.BlockSpec(memory_space=pltpu.SMEM), hbm],
        out_specs=(vmem, vmem),
        scratch_shapes=[
            pltpu.VMEM(offsets.shape, jnp.int32),
            pltpu.VMEM((parts, az_rows, rg_cols + 2 * LANES), jnp.bfloat16),
            pltpu.VMEM((2 * TAPS - 1, az_rows, LANES), jnp.float32),
            pltpu.VMEM((group, pair_count, az_rows, 2 * looks), jnp.float32),
            pltpu.VMEM((slots, az_rows, 2 * looks), jnp.float32),
        ]
        + [pltpu.VMEM((slots, parts, az_rows, width), jnp.bfloat16) for width in widths]
        + [pltpu.VMEM((group, parts, az_rows, width), jnp.bfloat16) for width in widths]
        + [pltpu.VMEM((4 * width, 2 * looks), jnp.bfloat16) for width in widths]
        + [pltpu.VMEM((2 * width, 2 * looks), jnp.bfloat16) for width in widths]
        + [
            dma(()),
            dma(()),
            dma((CHUNKS,)),
            dma((CHUNKS, group)),
            dma((CHUNKS, group)),
            dma((CHUNKS, MAXGAP)),
            dma((CHUNKS, MAXGAP)),
            dma((CHUNKS, MAXGAP)),
            dma((CHUNKS, MAXGAP)),
        ],
        compiler_params=pltpu.CompilerParams(
            collective_id=0, has_side_effects=True, vmem_limit_bytes=60 * 1024 * 1024
        ),
    )(offsets, partners.T, slc)


def solution(mesh):
    return jax.shard_map(
        functools.partial(body, mesh.shape["tile"]),
        mesh=mesh,
        in_specs=(P(("acq", "tile"), None, None, None), P(), P()),
        out_specs=(P(None, "acq", None, None, "tile"), P("acq", None, None, "tile")),
        check_vma=False,
    )
```

time: 81.3 us -> 69.9 us (0.86)
  the two profiles are of different devices: /device:TPU:1 before, /device:TPU:9 now
where the time goes in v1:
time: 69.9 us; the launch traced here: 69.7 us
  Pallas kernels  65.5 us (94%)
  local copies, waits for them, and re-layouts  3.55 us (5%)
    pallas_call x1, Pallas kernels, body(): pl.pallas_call(kernel, out_shape=(jax.ShapeDtypeStruct((2, group, pair_co...  65.5 us
    unnamed x2, local copies, waits for them, and re-layouts  3.55 us

profile of v1, /device:TPU:9, one launch (start us, length us, event | category | flops | bytes accessed | tf_op | source)
XLA Modules:
  0.0 69.7 jit_solution(5385305508740271131)
XLA Ops:
  0.6 65.5 %shard_map.50 = (f32[2,8,4,16,64]{4,3,2,1,0:T(8,128)}, f32[8,4,16,64]{3,2,1,0:T(8,128)}) custom-call(s32[32,64]{1,0:T(8,128)} %offsets_ref.1, s32[4,32]{1,0:T(4,128)} %bitcast.1, bf16[1,2,64,8192]{3,2,1,0:T(8,128)(2,1)} %slc_ref.1), custom_call_target="tpu_custom_call" | custom-call | tf_op jit(solution)/shard_map/pallas_call | solution.py:373
  66.1 1.9 %copy.7 = f32[2,8,4,16,64]{4,3,2,1,0:T(8,128)} copy(f32[2,8,4,16,64]{4,3,2,1,0:T(8,128)} %get-tuple-element.4) | data formatting | bytes 524288
  68.0 1.7 %copy.8 = f32[8,4,16,64]{3,2,1,0:T(8,128)} copy(f32[8,4,16,64]{3,2,1,0:T(8,128)} %get-tuple-element.5) | data formatting | bytes 262144

commit v2 on v1

--- a/solution.py
+++ b/solution.py
@@ -16,7 +16,7 @@
 SHARES = (1, 1, 1, 1)
 CHUNKS = len(SHARES)
 EARLY = 1
-OWNERS = 4
+OWNERS = 8
 DEVICE = pl.DeviceIdType.MESH
 
 
@@ -269,17 +269,17 @@
 
         def powers(index, carry):
             squares = []
-            for k in range(4):
-                image = images[index * 4 + k]
+            for k in range(slots // 2):
+                image = images[index * (slots // 2) + k]
                 squares.append(jnp.concatenate([image[0] * image[0], image[1] * image[1]], axis=1))
             pooled = jnp.dot(
                 jnp.concatenate(squares, axis=0), pool_power[chunk][...], preferred_element_type=jnp.float32
-            ).reshape(4, az_rows, 2 * looks)
-            span = pl.ds(index * 4, 4)
+            ).reshape(slots // 2, az_rows, 2 * looks)
+            span = pl.ds(index * (slots // 2), slots // 2)
             power_sum[span] = pooled if chunk == 0 else power_sum[span] + pooled
             return carry
 
-        lax.fori_loop(0, slots // 4, powers, 0)
+        lax.fori_loop(0, 2, powers, 0)
 
         def crosses(index, carry):
             blocks = []

time: 69.9 us -> 68.7 us (0.983)
  Pallas kernels: 65.5 us -> 64.2 us
    pallas_call x1, Pallas kernels: 65.5 us -> 64.2 us  [body(): pl.pallas_call(kernel, out_shape=(jax.ShapeDtypeStruct((2, group, pair_co...]
where the time goes in v2:
time: 68.7 us; the launch traced here: 68.4 us
  Pallas kernels  64.2 us (93%)
  local copies, waits for them, and re-layouts  3.55 us (5%)
    pallas_call x1, Pallas kernels, body(): pl.pallas_call(kernel, out_shape=(jax.ShapeDtypeStruct((2, group, pair_co...  64.2 us
    unnamed x2, local copies, waits for them, and re-layouts  3.55 us

profile of v2, /device:TPU:9, one launch (start us, length us, event | category | flops | bytes accessed | tf_op | source)
XLA Modules:
  0.0 68.4 jit_solution(8121699029212302285)
XLA Ops:
  0.6 64.2 %shard_map.50 = (f32[2,8,4,16,64]{4,3,2,1,0:T(8,128)}, f32[8,4,16,64]{3,2,1,0:T(8,128)}) custom-call(s32[32,64]{1,0:T(8,128)} %offsets_ref.1, s32[4,32]{1,0:T(4,128)} %bitcast.1, bf16[1,2,64,8192]{3,2,1,0:T(8,128)(2,1)} %slc_ref.1), custom_call_target="tpu_custom_call" | custom-call | tf_op jit(solution)/shard_map/pallas_call | solution.py:373
  64.9 1.9 %copy.7 = f32[2,8,4,16,64]{4,3,2,1,0:T(8,128)} copy(f32[2,8,4,16,64]{4,3,2,1,0:T(8,128)} %get-tuple-element.4) | data formatting | bytes 524288
  66.7 1.7 %copy.8 = f32[8,4,16,64]{3,2,1,0:T(8,128)} copy(f32[8,4,16,64]{3,2,1,0:T(8,128)} %get-tuple-element.5) | data formatting | bytes 262144
